TPU v7x, 128 devices: a whole 4x4x4 slice. The times are simulated.
128 devices in a mesh: tp: 8 (over z, core), kv: 16 (over x, y).
Axes of the slice: x: 4, y: 4, z: 4, core: 2. Of those that a mesh axis runs over, the one named last changes fastest.
Arguments:
- tokens: bfloat16 [64, 8192], P(None, 'kv'), may hold values from -6 to 6
- gain: float32 [8192], P('kv'), may hold values from 0.1 to 1.9
- w_qkv: bfloat16 [8192, 8, 1280], P('kv', 'tp'), may hold values from -0.0625 to 0.0625
- w_out: bfloat16 [8, 1024, 8192], P('tp', None, 'kv'), may hold values from -0.0625 to 0.0625
- k_cache: bfloat16 [8, 160, 4096, 128], P('tp', 'kv')
- v_cache: bfloat16 [8, 160, 4096, 128], P('tp', 'kv'), may hold values from -12 to 12
- lengths: int32 [64], replicated, may hold values from 1 to 131072, as said below
- block_table: int32 [160, 2], P('kv'), may hold values from -1 to 63, as said below
Outputs:
- attn_proj: bfloat16 [64, 8192], P(None, 'kv')
Inputs may be any that keep to these rules, and one draw needn't show every extreme that they name: `lengths`: every sequence has at least one cached token; exactly one sequence has 131072. `block_table`: entry [s, 0] is the sequence whose block sits in slot s and [s, 1] the block's place p in it (its tokens 4096 * p to 4096 * p + 4095); both are -1 for an empty slot. Each block that holds at least one cached token of a sequence sits in exactly one slot, and no other block is stored. On each index of kv the used slots come first; on some index all 10 slots are used.
All inputs are finite; a program needn't handle non-finite values.
Results may differ from a plain program's by a relative error of at most 0.0065.
The roundings to bfloat16 on the way count: a program that leaves them out, or rounds other values in their place, can miss the bound.
Values may be sent and summed in bfloat16 or wider, within the bound.
A program may use at most 128 MiB of HBM per device.

v0:
```python
import jax
import jax.numpy as jnp
from jax import lax
from jax.sharding import PartitionSpec as P

D = 8192
HD = 128
G = 8


epsilon = 1e-05
floor_score = -1e30


def combine(earlier, later):
    first_top, first_sums, first_weighted = earlier
    second_top, second_sums, second_weighted = later
    highest = jnp.maximum(first_top, second_top)
    first_factor = jnp.exp(first_top - highest)
    second_factor = jnp.exp(second_top - highest)
    merged_sums = first_sums * first_factor + second_sums * second_factor
    merged_weighted = (
        first_weighted * first_factor[..., None] + second_weighted * second_factor[..., None]
    )
    return (highest, merged_sums, merged_weighted)


def attend_slots(queries, lengths, key_store, value_store, slot_table, live_count, carry_init):
    block_length = key_store.shape[2]
    score_scale = key_store.shape[3] ** (-0.5)
    offsets = jnp.arange(block_length, dtype=jnp.int32)

    def visit(slot_index, running):
        owner_row = jnp.maximum(slot_table[slot_index, 0], 0)
        start_token = slot_table[slot_index, 1] * block_length
        query_rows = lax.dynamic_index_in_dim(queries, owner_row, 0, keepdims=False)
        key_block = lax.dynamic_index_in_dim(key_store, slot_index, 1, keepdims=False)
        value_block = lax.dynamic_index_in_dim(value_store, slot_index, 1, keepdims=False)
        scores = (
            jnp.einsum("hgd,hjd->hgj", query_rows, key_block, preferred_element_type=jnp.float32)
            * score_scale
        )
        visible = start_token + offsets < lengths[owner_row]
        scores = jnp.where(visible[None, None, :], scores, floor_score)
        block_top = jnp.max(scores, axis=-1)
        weights = jnp.exp(scores - block_top[..., None])
        block_total = jnp.sum(weights, axis=-1)
        block_out = jnp.einsum(
            "hgj,hjd->hgd",
            weights.astype(jnp.bfloat16),
            value_block,
            preferred_element_type=jnp.float32,
        )
        current = tuple(
            (
                lax.dynamic_index_in_dim(state_part, owner_row, 0, keepdims=True)
                for state_part in running
            )
        )
        updated = combine(current, (block_top[None], block_total[None], block_out[None]))
        return tuple(
            (
                lax.dynamic_update_index_in_dim(state_part, new_part, owner_row, 0)
                for state_part, new_part in zip(running, updated)
            )
        )

    return lax.fori_loop(0, live_count, visit, carry_init)


def finish(cache_top, weight_sums, weighted, queries, new_keys, new_values):
    score_scale = queries.shape[-1] ** (-0.5)
    own_scores = (
        jnp.sum(queries.astype(jnp.float32) * new_keys.astype(jnp.float32)[:, :, None, :], axis=-1)
        * score_scale
    )
    highest = jnp.maximum(cache_top, own_scores)
    cache_factor = jnp.exp(cache_top - highest)
    own_weight = jnp.exp(own_scores - highest)
    denominator = weight_sums * cache_factor + own_weight
    numerator = (
        weighted * cache_factor[..., None]
        + own_weight[..., None] * new_values.astype(jnp.float32)[:, :, None, :]
    )
    return (numerator / denominator[..., None]).astype(jnp.bfloat16)


def per_device(tokens, gain, w_qkv, w_out, k_cache, v_cache, lengths, block_table):
    row_count = tokens.shape[0]
    wide_tokens = tokens.astype(jnp.float32)
    squares = lax.psum(jnp.sum(wide_tokens * wide_tokens, axis=1), "kv")
    normed = (wide_tokens * lax.rsqrt(squares / D + epsilon)[:, None] * gain[None, :]).astype(
        jnp.bfloat16
    )
    local_heads = w_qkv.shape[1]
    partial_proj = jnp.dot(
        normed,
        w_qkv.reshape(w_qkv.shape[0], local_heads * w_qkv.shape[2]),
        preferred_element_type=jnp.float32,
    )
    projected = lax.psum(partial_proj, "kv").astype(jnp.bfloat16)
    projected = projected.reshape(row_count, local_heads, G + 2, HD)
    queries = projected[:, :, :G]
    new_keys = projected[:, :, G]
    new_values = projected[:, :, G + 1]
    start_state = (
        jnp.full((row_count, local_heads, G), floor_score, jnp.float32),
        jnp.zeros((row_count, local_heads, G), jnp.float32),
        jnp.zeros((row_count, local_heads, G, HD), jnp.float32),
    )
    live_total = jnp.sum((block_table[:, 0] >= 0).astype(jnp.int32))
    running = attend_slots(queries, lengths, k_cache, v_cache, block_table, live_total, start_state)
    highest = lax.pmax(running[0], "kv")
    factors = jnp.exp(running[0] - highest)
    weight_sums, weighted = lax.psum((running[1] * factors, running[2] * factors[..., None]), "kv")
    attended = finish(highest, weight_sums, weighted, queries, new_keys, new_values)
    flattened = attended.reshape(row_count, local_heads * G * HD)
    head_terms = jnp.dot(
        flattened,
        w_out.reshape(local_heads * G * HD, w_out.shape[2]),
        preferred_element_type=jnp.float32,
    )
    return lax.psum(head_terms, "tp").astype(jnp.bfloat16)


def solution(mesh):
    placed = (
        P(None, "kv"),
        P("kv"),
        P("kv", "tp", None),
        P("tp", None, "kv"),
        P("tp", "kv", None, None),
        P("tp", "kv", None, None),
        P(),
        P("kv", None),
    )
    return jax.shard_map(
        per_device, mesh=mesh, in_specs=placed, out_specs=P(None, "kv"), check_vma=False
    )
```

profile of v0, /device:TPU:1, one launch (start us, length us, event | category | flops | bytes accessed | tf_op | source)
XLA Modules:
  0.0 398.8 jit_solution(10366553633407420208)
XLA Ops:
  6.5 1.5 fusion.38
  9.0 34.3 %psum.35 = f32[64]{0:T(128)S(1)} all-reduce(f32[64]{0:T(128)S(1)} %fusion.28), channel_id=1, replica_groups=mesh['tp'=8,'kv'=16] {'kv'}, use_global_device_ids=true, to_apply=%region_2.0 | all-reduce | flops 64 | bytes 512 | tf_op jit(solution)/shard_map/psum | solution.py:91
  44.6 59.1 %all-reduce.5 = bf16[64,1280]{1,0:T(8,128)(2,1)S(1)} all-reduce(f32[64,1280]{1,0:T(8,128)S(1)} %fusion.24), channel_id=1, replica_groups=mesh['tp'=8,'kv'=16] {'kv'}, use_global_device_ids=true, to_apply=%region_3.0 | all-reduce | flops 81920 | bytes 491520 | tf_op jit(solution)/shard_map/psum | solution.py:101
  103.9 88.6 %while.15 = (s32[]{:T(128)}, f32[64,1,8]{2,1,0:T(1,128)S(1)}, f32[64,1,8]{2,1,0:T(1,128)S(1)}, f32[64,1,8,128]{3,2,1,0:T(8,128)S(1)}, s32[]{:T(128)}, /*index=5*...) while((s32[]{:T(128)}, f32[64,1,8]{2,1,0:T(1,128)S(1)}, ...), condition=%wide.region_7.8_spmd.clone, body=%wide.region_4.7_spmd.clone.sunk | while | flops 17017896 | bytes 2515811 | solution.py:68
  104.6 1.4 constant_dynamic-slice_fusion.6
  109.1 1.7 fusion.53
  111.1 1.5 fusion.56
  117.9 1.7 fusion.53
  119.9 1.5 fusion.56
  122.2 1.4 constant_dynamic-slice_fusion.6
  126.7 1.7 fusion.53
  128.7 1.5 fusion.56
  130.9 1.4 constant_dynamic-slice_fusion.6
  135.5 1.7 fusion.53
  137.5 1.5 fusion.56
  139.7 1.4 constant_dynamic-slice_fusion.6
  144.3 1.7 fusion.53
  146.3 1.5 fusion.56
  153.1 1.7 fusion.53
  155.1 1.5 fusion.56
  161.9 1.7 fusion.53
  163.9 1.5 fusion.56
  170.7 1.7 fusion.53
  172.6 1.5 fusion.56
  179.5 1.7 fusion.53
  181.4 1.5 fusion.56
  188.2 1.7 fusion.53
  190.2 1.5 fusion.56
  192.5 56.7 %pmax.7 = f32[64,1,8]{2,1,0:T(1,128)S(1)} all-reduce(f32[64,1,8]{2,1,0:T(1,128)S(1)} %get-tuple-element.66), channel_id=1, replica_groups=mesh['tp'=8,'kv'=16] {'kv'}, use_global_device_ids=true, to_apply=%region_8.9 | all-reduce | flops 512 | bytes 4096 | tf_op jit(solution)/shard_map/pmax | solution.py:113
  250.3 55.7 %psum.38 = f32[64,1,8]{2,1,0:T(1,128)S(1)} all-reduce(f32[64,1,8]{2,1,0:T(1,128)S(1)} %bitcast.104), channel_id=1, replica_groups=mesh['tp'=8,'kv'=16] {'kv'}, use_global_device_ids=true, to_apply=%region_11.12 | all-reduce | flops 512 | bytes 4096 | tf_op jit(solution)/shard_map/psum | solution.py:115
  306.0 59.7 %all-reduce.4.cloned.1.call-done = f32[64,1,8,128]{3,2,1,0:T(8,128)} async-done(((f32[64,1,8,128]{3,2,1,0:T(8,128)}), f32[64,1,8,128]{3,2,1,0:T(8,128)}) %all-reduce.4.cloned.1.call-update) | async-done | bytes 262160 | tf_op jit(solution)/shard_map/psum | solution.py:115
  367.3 24.7 %all-reduce.6 = bf16[64,512]{1,0:T(8,128)(2,1)} all-reduce(f32[64,512]{1,0:T(8,128)S(1)} %fusion.26), channel_id=1, replica_groups=mesh['tp'=8,'kv'=16] {'tp'}, use_global_device_ids=true, to_apply=%region_12.13 | all-reduce | flops 32768 | bytes 196608 | tf_op jit(solution)/shard_map/psum | solution.py:123
  (68 shorter events, 35.4 us)
Async XLA Ops:
  6.5 36.8 %copy-start = (bf16[512,1,1280]{2,0,1:T(8,128)(2,1)S(1)}, bf16[512,1,1280]{2,0,1:T(8,128)(2,1)}, u32[]{:S(2)}) copy-start(bf16[512,1,1280]{2,0,1:T(8,128)(2,1)} %param.12) | copy-start | bytes 3932164
  6.5 360.4 %copy-start.1 = (bf16[1,1024,512]{2,1,0:T(8,128)(2,1)S(1)}, bf16[1,1024,512]{2,1,0:T(8,128)(2,1)}, u32[]{:S(2)}) copy-start(bf16[1,1024,512]{2,1,0:T(8,128)(2,1)} %param.13) | copy-start | bytes 3145732
  6.5 359.2 %all-reduce.4.cloned.1.call-start = ((), (), s32[]{:S(2)}) async-start(), calls=%async_computation | async-start | bytes 524288 | tf_op jit(solution)/shard_map/psum | solution.py:115
Sparse Core Ops, SparseCore 0:
  250.2 115.4 all-reduce.3
where the time goes:
time: 403 us; the launch traced here: 399 us
  blocking collectives  230 us (57%)
  waiting for transfers between devices  59.7 us (15%)
  matrix products  34 us (8%)
  local copies, waits for them, and re-layouts  27.3 us (7%)
  loops' own time  20.1 us (5%)
  other arithmetic  13.7 us (3%)
  between operations  13.5 us (3%)
    psum x1, waiting for transfers between devices, per_device(): lax.psum((running[1] * factors, running[2] * factors[..., None]), 'kv')  59.7 us
    psum x1, blocking collectives, per_device(): projected = lax.psum(partial_proj, 'kv').astype(jnp.bfloat16)  59.1 us
    pmax x1, blocking collectives, per_device(): highest = lax.pmax(running[0], 'kv')  56.7 us
    psum x1, blocking collectives, per_device(): lax.psum((running[1] * factors, running[2] * factors[..., None]), 'kv')  55.7 us
    psum x1, blocking collectives, per_device(): squares = lax.psum(jnp.sum(wide_tokens * wide_tokens, axis=1), 'kv')  34.3 us
    psum x1, blocking collectives, per_device(): return lax.psum(head_terms, 'tp').astype(jnp.bfloat16)  24.7 us
    another operation x1, loops' own time, attend_slots(): return lax.fori_loop(0, live_count, visit, carry_init)  20.1 us
    dot_general x10, matrix products, visit(): jnp.einsum('hgd,hjd->hgj', query_rows, key_block, preferred_element_type=...  17.2 us
  transfers between devices with their start and end apart: 1, of which 1 were waited for; matrix products, arithmetic and copies ran while one was open for 0% of the time, Pallas kernels for 0%

commit v1 on v0

v1 whole, which is shorter than its diff:
```python
import functools

import jax
import jax.numpy as jnp
from jax import lax
from jax.experimental import pallas as pl
from jax.experimental.pallas import tpu as pltpu
from jax.sharding import PartitionSpec as P

D = 8192
HD = 128
G = 8
ROWS = 64
SLOTS = 10
ENTRIES = G + 2
BLK = 4096
SIDE = 4
KV = SIDE * SIDE
PEERS = KV - 1
HALF = 256

EPSILON = 1e-05
FLOOR = -1e30
SCALE = HD ** (-0.5)

MESH = pl.DeviceIdType.MESH
F32 = jnp.float32
BF16 = jnp.bfloat16
NT = (((1,), (1,)), ((), ()))

CHUNKS = ((0, 4, 40), (4, 4, 40), (8, 2, 24))


def ring_distance(step):
    return min(step, SIDE - step)


OFFSETS = sorted(
    [(a, b) for a in range(SIDE) for b in range(SIDE) if (a, b) != (0, 0)],
    key=lambda m: -(ring_distance(m[0]) + ring_distance(m[1])),
)


def wait_bytes(ref, sem):
    pltpu.make_async_copy(ref, ref, sem).wait()


def kernel(
    tokens_hbm,
    gain_hbm,
    w_qkv_hbm,
    w_out_hbm,
    k_hbm,
    v_hbm,
    lengths,
    table,
    out_ref,
    tokens_v,
    gain_v,
    w_qkv,
    w_out,
    k_v,
    v_v,
    first_all,
    send0,
    send1,
    send2,
    recv0,
    recv1,
    recv2,
    query_rows,
    outs_all,
    stats_all,
    outs_wide,
    half_send,
    half_recv,
    z_all,
    done_send,
    done_recv,
    load_sem,
    kv_sem,
    send_sem,
    recv_sem,
):
    me = lax.axis_index("kv")
    my_x, my_y = me // SIDE, me % SIDE
    tp = lax.axis_index("tp")
    my_z, core = tp // 2, tp % 2

    def ahead(offset):
        return {"kv": ((my_x + offset[0]) % SIDE) * SIDE + (my_y + offset[1]) % SIDE}

    def behind(offset):
        return ahead(((SIDE - offset[0]) % SIDE, (SIDE - offset[1]) % SIDE))

    sibling = {"tp": my_z * 2 + (1 - core)}
    z_peers = [{"tp": ((my_z + step) % SIDE) * 2 + core} for step in (2, 1, 3)]

    barrier = pltpu.get_barrier_semaphore()
    for offset in OFFSETS:
        pl.semaphore_signal(barrier, inc=1, device_id=ahead(offset), device_id_type=MESH)
    for peer in z_peers + [sibling]:
        pl.semaphore_signal(barrier, inc=1, device_id=peer, device_id_type=MESH)

    loads = [
        pltpu.make_async_copy(tokens_hbm, tokens_v, load_sem.at[0]),
        pltpu.make_async_copy(gain_hbm, gain_v, load_sem.at[1]),
        pltpu.make_async_copy(w_qkv_hbm, w_qkv, load_sem.at[2]),
        pltpu.make_async_copy(w_out_hbm, w_out, load_sem.at[3]),
    ]
    k_loads, v_loads = [], []
    for pair in range(SLOTS // 2):
        part = pl.ds(2 * pair, 2)
        k_loads.append(pltpu.make_async_copy(k_hbm.at[part], k_v.at[part], kv_sem.at[0, pair]))
        v_loads.append(pltpu.make_async_copy(v_hbm.at[part], v_v.at[part], kv_sem.at[1, pair]))
    for load in loads[:3]:
        load.start()
    for pair in range(SLOTS // 2):
        k_loads[pair].start()
        v_loads[pair].start()
    loads[3].start()

    sub = lax.broadcasted_iota(jnp.int32, (8, HD), 0)
    lane = lax.broadcasted_iota(jnp.int32, (8, HD), 1)

    loads[0].wait()
    tokens = tokens_v[...].astype(F32)
    squares = jnp.sum(tokens * tokens, axis=1, keepdims=True)
    tile = jnp.zeros((8, HD), F32)
    for k in range(ROWS // 8):
        tile = jnp.where(lane == k, squares[8 * k : 8 * k + 8], tile)
    first_all[PEERS, 0:8, :] = tile
    for c, (start, count, _) in enumerate(CHUNKS):
        owners = jnp.full((8, HD), -1, jnp.int32)
        for s in range(count):
            owners = jnp.where(sub % count == s, table[0, start + s], owners)
        first_all[PEERS, 8 + 8 * c : 16 + 8 * c, :] = owners.astype(F32)
    owners = jnp.full((8, HD), -1, jnp.int32)
    for s in range(SLOTS):
        owners = jnp.where(lane == s, table[0, s], owners)
    first_all[PEERS, 32:40, :] = owners.astype(F32)

    pl.semaphore_wait(barrier, PEERS + 4)

    def send(phase, src, dst, peer):
        pltpu.make_async_remote_copy(
            src_ref=src,
            dst_ref=dst,
            send_sem=send_sem.at[phase],
            recv_sem=recv_sem.at[phase],
            device_id=peer,
            device_id_type=MESH,
        ).start()

    others = pl.ds(0, PEERS)

    for j, offset in enumerate(OFFSETS):
        send(0, first_all.at[PEERS], first_all.at[j], ahead(offset))
    loads[1].wait()
    loads[2].wait()
    wait_bytes(first_all.at[others], recv_sem.at[0])

    squares = first_all[0, 0:8, :]
    for j in range(1, KV):
        squares = squares + first_all[j, 0:8, :]
    inverse = lax.rsqrt(squares / D + EPSILON)
    gains = gain_v[...]
    normed = jnp.concatenate(
        [tokens[8 * k : 8 * k + 8] * inverse[:, k : k + 1] * gains for k in range(ROWS // 8)], axis=0
    ).astype(BF16)
    partial = jnp.dot(normed, w_qkv[...], preferred_element_type=F32)
    high = partial.astype(BF16)
    rest = partial - high.astype(F32)
    middle = rest.astype(BF16)
    low = (rest - middle.astype(F32)).astype(BF16)
    stacked = jnp.concatenate([high, middle, low, jnp.zeros_like(low)], axis=0)

    row_of_lane = lax.broadcasted_iota(jnp.int32, (KV * 8, HD), 1)
    row_number = (row_of_lane % ROWS).astype(F32)
    sub3 = lax.broadcasted_iota(jnp.int32, (KV, 8, HD), 1)
    sends = (send0, send1, send2)
    recvs = (recv0, recv1, recv2)
    for c, (start, count, rows) in enumerate(CHUNKS):
        owners = first_all[:, 8 + 8 * c : 16 + 8 * c, :].reshape(KV * 8, HD)
        hit = jnp.where(owners == row_number, 1.0, 0.0)
        pick = jnp.concatenate([hit, jnp.where(row_of_lane < ROWS, hit, 0.0)], axis=1).astype(BF16)
        packed = jnp.dot(pick, stacked, preferred_element_type=F32).reshape(KV, 8, ENTRIES * HD)
        per_tile = 8 // count
        for k in range(rows // 8):
            tile = packed[:, :, per_tile * k * HD : (per_tile * k + 1) * HD]
            for e in range(1, per_tile):
                entry = per_tile * k + e
                if entry < ENTRIES:
                    tile = jnp.where(
                        sub3 >= e * count, packed[:, :, entry * HD : (entry + 1) * HD], tile
                    )
            sends[c][:, 8 * k : 8 * k + 8, :] = tile
        for j, offset in enumerate(OFFSETS):
            send(1 + c, sends[c].at[j], recvs[c].at[j], behind(offset))

    sub16 = lax.broadcasted_iota(jnp.int32, (16, HD), 0)
    column = lax.broadcasted_iota(jnp.int32, (16, 1), 0)
    position = lax.broadcasted_iota(jnp.int32, (16, BLK), 1)
    stats = jnp.zeros((8, HD), F32)

    for c, (start, count, rows) in enumerate(CHUNKS):
        wait_bytes(recvs[c].at[others], recv_sem.at[1 + c])
        total = sends[c][PEERS]
        for j in range(PEERS):
            total = total + recvs[c][j]
        total = total.astype(BF16).astype(F32)
        per_tile = 8 // count
        for entry in range(ENTRIES):
            row = entry * count
            query_rows[pl.ds(16 * start + entry, count, stride=16), :] = total[row : row + count]

        for pair in range(start // 2, (start + count) // 2):
            a, b = 2 * pair, 2 * pair + 1
            k_loads[pair].wait()
            v_loads[pair].wait()
            queries = jnp.concatenate(
                [query_rows[16 * a : 16 * a + 8, :], query_rows[16 * b : 16 * b + 8, :]], axis=0
            )
            new_keys = jnp.where(
                sub16 < 8, query_rows[16 * a + 8 : 16 * a + 9, :], query_rows[16 * b + 8 : 16 * b + 9, :]
            )
            new_values = jnp.where(
                sub16 < 8, query_rows[16 * a + 9 : 16 * a + 10, :], query_rows[16 * b + 9 : 16 * b + 10, :]
            )
            left = jnp.concatenate(
                [jnp.where(sub16 < 8, queries, 0.0), jnp.where(sub16 < 8, 0.0, queries)], axis=1
            ).astype(BF16)
            keys = jnp.concatenate([k_v[a], k_v[b]], axis=1)
            scores = lax.dot_general(left, keys, NT, preferred_element_type=F32) * SCALE
            limit_a = lengths[jnp.maximum(table[0, a], 0)] - BLK * table[1, a]
            limit_b = lengths[jnp.maximum(table[0, b], 0)] - BLK * table[1, b]
            limit = jnp.where(column < 8, limit_a, limit_b)
            scores = jnp.where(position < limit, scores, FLOOR)
            top = jnp.max(scores, axis=1, keepdims=True)
            weights = jnp.exp(scores - top)
            block_total = jnp.sum(weights, axis=1, keepdims=True)
            values = jnp.concatenate([v_v[a], v_v[b]], axis=1)
            both = jnp.dot(weights.astype(BF16), values, preferred_element_type=F32)
            block_out = jnp.where(sub16 < 8, both[:, :HD], both[:, HD:])

            is_first = jnp.where(column < 8, table[1, a], table[1, b]) == 0
            own = jnp.sum(queries * new_keys, axis=1, keepdims=True) * SCALE
            own = jnp.where(is_first, own, FLOOR)
            highest = jnp.maximum(top, own)
            factor = jnp.exp(top - highest)
            own_weight = jnp.where(is_first, jnp.exp(own - highest), 0.0)
            slot_total = block_total * factor + own_weight
            slot_out = (block_out * factor + own_weight * new_values) / slot_total
            outs_all[PEERS, 16 * pair : 16 * pair + 16, :] = slot_out.astype(BF16)
            for s, part in ((a, slice(0, 8)), (b, slice(8, 16))):
                stats = jnp.where(lane == s, highest[part], stats)
                stats = jnp.where(lane == 16 + s, slot_total[part], stats)
        part = pl.ds(8 * start, 8 * count)
        for j, offset in enumerate(OFFSETS):
            send(4 + c, outs_all.at[PEERS, part], outs_all.at[j, part], ahead(offset))
    stats_all[PEERS] = stats
    for j, offset in enumerate(OFFSETS):
        send(7, stats_all.at[PEERS], stats_all.at[j], ahead(offset))

    def side_by_side(tiles, shift):
        near = jnp.full((8, HD), -1.0, F32)
        far = jnp.full((8, HD), -1.0, F32)
        for j in range(KV):
            at = SLOTS * j
            moved = pltpu.roll(tiles(j), (at - shift) % HD, 1)
            if at < HD:
                near = jnp.where((lane >= at) & (lane < at + SLOTS), moved, near)
            if at + SLOTS > HD:
                far = jnp.where((lane >= at - HD) & (lane < at + SLOTS - HD), moved, far)
        return jnp.concatenate([near, far], axis=1)

    owners = side_by_side(lambda j: first_all[j, 32:40, :], 0)
    belongs = lax.broadcasted_iota(jnp.int32, (ROWS, 2 * HD), 0).astype(F32) == owners[0:1]

    wait_bytes(stats_all.at[others], recv_sem.at[7])
    tops = side_by_side(lambda j: stats_all[j], 0)
    totals = side_by_side(lambda j: stats_all[j], 16)
    shares = []
    for g in range(G):
        masked = jnp.where(belongs, tops[g : g + 1], -3e38)
        highest = jnp.max(masked, axis=1, keepdims=True)
        share = jnp.where(belongs, jnp.exp(masked - highest) * totals[g : g + 1], 0.0)
        share = share / jnp.sum(share, axis=1, keepdims=True)
        upper = share.astype(BF16)
        lower = (share - upper.astype(F32)).astype(BF16)
        shares.append(jnp.concatenate([upper, lower], axis=0))

    for c, (start, count, rows) in enumerate(CHUNKS):
        wait_bytes(outs_all.at[others, pl.ds(8 * start, 8 * count)], recv_sem.at[4 + c])
    outs_wide[...] = outs_all[...].astype(F32).reshape(KV * SLOTS * G, HD)
    attended = []
    for g in range(G):
        slots = outs_wide[pl.ds(g, KV * SLOTS, stride=G), :].astype(BF16)
        slots = jnp.concatenate([slots, jnp.zeros((2 * HD - KV * SLOTS, HD), BF16)], axis=0)
        both = jnp.dot(shares[g], slots, preferred_element_type=F32)
        attended.append((both[:ROWS] + both[ROWS:]).astype(BF16))
    attended = jnp.concatenate(attended, axis=1)

    loads[3].wait()
    mine = pl.ds(pl.multiple_of(core * HALF, HALF), HALF)
    theirs = pl.ds(pl.multiple_of((1 - core) * HALF, HALF), HALF)
    half_send[...] = jnp.dot(attended, w_out[:, theirs], preferred_element_type=F32)
    send(8, half_send, half_recv, sibling)
    own_half = jnp.dot(attended, w_out[:, mine], preferred_element_type=F32)
    wait_bytes(half_recv, recv_sem.at[8])
    z_all[my_z] = own_half + half_recv[...]
    for peer in z_peers:
        send(9, z_all.at[my_z], z_all.at[my_z], peer)
    wait_bytes(z_all.at[pl.ds(0, SIDE - 1)], recv_sem.at[9])
    done = (((z_all[0] + z_all[1]) + z_all[2]) + z_all[3]).astype(BF16)
    done_send[...] = done
    send(10, done_send, done_recv, sibling)
    out_ref[:, mine] = done
    wait_bytes(done_recv, recv_sem.at[10])
    out_ref[:, theirs] = done_recv[...]

    wait_bytes(first_all.at[others], send_sem.at[0])
    for c, (start, count, rows) in enumerate(CHUNKS):
        wait_bytes(sends[c].at[others], send_sem.at[1 + c])
        wait_bytes(outs_all.at[others, pl.ds(8 * start, 8 * count)], send_sem.at[4 + c])
    wait_bytes(stats_all.at[others], send_sem.at[7])
    wait_bytes(half_send, send_sem.at[8])
    wait_bytes(z_all.at[pl.ds(0, SIDE - 1)], send_sem.at[9])
    wait_bytes(done_send, send_sem.at[10])


def per_device(tokens, gain, w_qkv, w_out, k_cache, v_cache, lengths, block_table):
    features = tokens.shape[1]
    anywhere = pl.BlockSpec(memory_space=pl.ANY)
    scalars = pl.BlockSpec(memory_space=pltpu.SMEM)
    return pl.pallas_call(
        kernel,
        out_shape=jax.ShapeDtypeStruct((ROWS, features), BF16),
        in_specs=[anywhere] * 6 + [scalars] * 2,
        out_specs=pl.BlockSpec(memory_space=pltpu.VMEM),
        scratch_shapes=[
            pltpu.VMEM((ROWS, features), BF16),
            pltpu.VMEM((1, features), F32),
            pltpu.VMEM((features, ENTRIES * HD), BF16),
            pltpu.VMEM((G * HD, features), BF16),
            pltpu.VMEM((SLOTS, BLK, HD), BF16),
            pltpu.VMEM((SLOTS, BLK, HD), BF16),
            pltpu.VMEM((KV, 40, HD), F32),
        ]
        + [pltpu.VMEM((KV, rows, HD), F32) for _, _, rows in CHUNKS]
        + [pltpu.VMEM((PEERS, rows, HD), F32) for _, _, rows in CHUNKS]
        + [
            pltpu.VMEM((SLOTS * 16, HD), F32),
            pltpu.VMEM((KV, SLOTS * G, HD), BF16),
            pltpu.VMEM((KV, 8, HD), F32),
            pltpu.VMEM((KV * SLOTS * G, HD), F32),
            pltpu.VMEM((ROWS, HALF), F32),
            pltpu.VMEM((ROWS, HALF), F32),
            pltpu.VMEM((SIDE, ROWS, HALF), F32),
            pltpu.VMEM((ROWS, HALF), BF16),
            pltpu.VMEM((ROWS, HALF), BF16),
            pltpu.SemaphoreType.DMA((4,)),
            pltpu.SemaphoreType.DMA((2, SLOTS // 2)),
            pltpu.SemaphoreType.DMA((11,)),
            pltpu.SemaphoreType.DMA((11,)),
        ],
        compiler_params=pltpu.CompilerParams(
            collective_id=0, has_side_effects=True, vmem_limit_bytes=56 << 20
        ),
    )(
        tokens,
        gain.reshape(1, features),
        w_qkv.reshape(features, ENTRIES * HD),
        w_out.reshape(G * HD, features),
        k_cache.reshape(SLOTS, BLK, HD),
        v_cache.reshape(SLOTS, BLK, HD),
        lengths,
        block_table.T,
    )


def solution(mesh):
    placed = (
        P(None, "kv"),
        P("kv"),
        P("kv", "tp", None),
        P("tp", None, "kv"),
        P("tp", "kv", None, None),
        P("tp", "kv", None, None),
        P(),
        P("kv", None),
    )
    return jax.shard_map(
        per_device, mesh=mesh, in_specs=placed, out_specs=P(None, "kv"), check_vma=False
    )
```

time: 403 us -> 49.7 us (0.12)
  blocking collectives: 230 us -> 0 us
  waiting for transfers between devices: 59.7 us -> 0 us
  Pallas kernels: 0 us -> 48 us
  matrix products: 34 us -> 0 us
  local copies, waits for them, and re-layouts: 27.3 us -> 1.47 us
  loops' own time: 20.1 us -> 0 us
  other arithmetic: 13.7 us -> 0 us
  between operations: 13.5 us -> 0.01 us
    psum x4 -> x0, blocking collectives: 174 us -> none  [the longest x1 59.1 us: per_device(): projected = lax.psum(partial_proj, 'kv').astype(jnp.bfloat16)]
    psum x1 -> x0, waiting for transfers between devices: 59.7 us -> none  [per_device(): lax.psum((running[1] * factors, running[2] * factors[..., None]), 'kv')]
    pmax x1 -> x0, blocking collectives: 56.7 us -> none  [per_device(): highest = lax.pmax(running[0], 'kv')]
    pallas_call x0 -> x1, Pallas kernels: none -> 48 us  [per_device(): pl.pallas_call(kernel, out_shape=jax.ShapeDtypeStruct((ROWS, features), B...]
    dot_general x22 -> x0, matrix products: 34 us -> none  [the longest x10 17.2 us: visit(): jnp.einsum('hgd,hjd->hgj', query_rows, key_block, preferred_element_type=...]
    dynamic_slice x20 -> x0, local copies, waits for them, and re-layouts: 27.1 us -> none  [the longest x10 14.1 us: visit(): start_token = slot_table[slot_index, 1] * block_length]
    another operation x1 -> x0, loops' own time: 20.1 us -> none  [attend_slots(): return lax.fori_loop(0, live_count, visit, carry_init)]
    lt x10 -> x0, other arithmetic: 6.37 us -> none  [visit(): visible = start_token + offsets < lengths[owner_row]]
  transfers between devices with their start and end apart: 1 -> 0, of which waited for: 1 -> 0; matrix products, arithmetic and copies ran while one was open for 0% -> 0% of each run, Pallas kernels for 0% -> 0%
where the time goes in v1:
time: 49.7 us; the launch traced here: 49.5 us
  Pallas kernels  48 us (97%)
  local copies, waits for them, and re-layouts  1.47 us (3%)
    pallas_call x1, Pallas kernels, per_device(): pl.pallas_call(kernel, out_shape=jax.ShapeDtypeStruct((ROWS, features), B...  48 us
    unnamed x1, local copies, waits for them, and re-layouts  1.47 us

profile of v1, /device:TPU:1, one launch (start us, length us, event | category | flops | bytes accessed | tf_op | source)
XLA Modules:
  0.0 49.5 jit_solution(9855653500914246935)
XLA Ops:
  0.0 48.0 %shard_map.82 = bf16[64,512]{1,0:T(8,128)(2,1)} custom-call(bf16[64,512]{1,0:T(8,128)(2,1)} %tokens_hbm.1, f32[1,512]{1,0:T(1,128)} %bitcast.10, bf16[512,1280]{1,0:T(8,128)(2,1)} %bitcast.8, bf16[1024,512]{1,0:T(8,128)(2,1)} %bitcast.9, bf16[10,4096,128]{2,1,0:T(8,128)(2,1)} %bitcast.6, bf16[10,4096,128]{2,1,0:T(8,128)(2,1)} %bitcast.7, s32[64]{0:T(128)} %lengths.1, ...), custom_call_target="tpu_custom_call" | custom-call | tf_op jit(solution)/shard_map/pallas_call | solution.py:336
  48.0 1.5 %copy.10 = bf16[64,512]{1,0:T(8,128)(2,1)} copy(bf16[64,512]{1,0:T(8,128)(2,1)} %shard_map.82) | data formatting | bytes 131072

commit v2 on v1

--- a/solution.py
+++ b/solution.py
@@ -28,6 +28,10 @@
 BF16 = jnp.bfloat16
 NT = (((1,), (1,)), ((), ()))
 
+SQUARE_LANE = 8
+OWNER_LANE = 16
+
+EARLY_PAIRS = 3
 CHUNKS = ((0, 4, 40), (4, 4, 40), (8, 2, 24))
 
 
@@ -52,8 +56,8 @@
     w_out_hbm,
     k_hbm,
     v_hbm,
-    lengths,
-    table,
+    lengths_hbm,
+    table_hbm,
     out_ref,
     tokens_v,
     gain_v,
@@ -77,6 +81,8 @@
     z_all,
     done_send,
     done_recv,
+    lengths,
+    table,
     load_sem,
     kv_sem,
     send_sem,
@@ -107,18 +113,19 @@
         pltpu.make_async_copy(gain_hbm, gain_v, load_sem.at[1]),
         pltpu.make_async_copy(w_qkv_hbm, w_qkv, load_sem.at[2]),
         pltpu.make_async_copy(w_out_hbm, w_out, load_sem.at[3]),
+        pltpu.make_async_copy(table_hbm, table, load_sem.at[4]),
+        pltpu.make_async_copy(lengths_hbm, lengths, load_sem.at[5]),
     ]
     k_loads, v_loads = [], []
     for pair in range(SLOTS // 2):
         part = pl.ds(2 * pair, 2)
         k_loads.append(pltpu.make_async_copy(k_hbm.at[part], k_v.at[part], kv_sem.at[0, pair]))
         v_loads.append(pltpu.make_async_copy(v_hbm.at[part], v_v.at[part], kv_sem.at[1, pair]))
-    for load in loads[:3]:
+    for load in loads[:3] + loads[4:]:
         load.start()
-    for pair in range(SLOTS // 2):
+    for pair in range(EARLY_PAIRS):
         k_loads[pair].start()
         v_loads[pair].start()
-    loads[3].start()
 
     sub = lax.broadcasted_iota(jnp.int32, (8, HD), 0)
     lane = lax.broadcasted_iota(jnp.int32, (8, HD), 1)
@@ -126,19 +133,18 @@
     loads[0].wait()
     tokens = tokens_v[...].astype(F32)
     squares = jnp.sum(tokens * tokens, axis=1, keepdims=True)
-    tile = jnp.zeros((8, HD), F32)
+    loads[4].wait()
+    loads[5].wait()
+    owners = jnp.full((8, HD), -1, jnp.int32)
+    for slot in range(SLOTS):
+        owners = jnp.where(lane == OWNER_LANE + slot, table[0, slot], owners)
+    for c, (start, count, _) in enumerate(CHUNKS):
+        for s in range(count):
+            owners = jnp.where((lane == c) & (sub % count == s), table[0, start + s], owners)
+    tile = owners.astype(F32)
     for k in range(ROWS // 8):
-        tile = jnp.where(lane == k, squares[8 * k : 8 * k + 8], tile)
-    first_all[PEERS, 0:8, :] = tile
-    for c, (start, count, _) in enumerate(CHUNKS):
-        owners = jnp.full((8, HD), -1, jnp.int32)
-        for s in range(count):
-            owners = jnp.where(sub % count == s, table[0, start + s], owners)
-        first_all[PEERS, 8 + 8 * c : 16 + 8 * c, :] = owners.astype(F32)
-    owners = jnp.full((8, HD), -1, jnp.int32)
-    for s in range(SLOTS):
-        owners = jnp.where(lane == s, table[0, s], owners)
-    first_all[PEERS, 32:40, :] = owners.astype(F32)
+        tile = jnp.where(lane == SQUARE_LANE + k, squares[8 * k : 8 * k + 8], tile)
+    first_all[PEERS] = tile
 
     pl.semaphore_wait(barrier, PEERS + 4)
 
@@ -160,13 +166,17 @@
     loads[2].wait()
     wait_bytes(first_all.at[others], recv_sem.at[0])
 
-    squares = first_all[0, 0:8, :]
+    for pair in range(EARLY_PAIRS, SLOTS // 2):
+        k_loads[pair].start()
+        v_loads[pair].start()
+    loads[3].start()
+    squares = first_all[0]
     for j in range(1, KV):
-        squares = squares + first_all[j, 0:8, :]
+        squares = squares + first_all[j]
     inverse = lax.rsqrt(squares / D + EPSILON)
     gains = gain_v[...]
     normed = jnp.concatenate(
-        [tokens[8 * k : 8 * k + 8] * inverse[:, k : k + 1] * gains for k in range(ROWS // 8)], axis=0
+        [tokens[8 * k : 8 * k + 8] * inverse[:, SQUARE_LANE + k : SQUARE_LANE + k + 1] * gains for k in range(ROWS // 8)], axis=0
     ).astype(BF16)
     partial = jnp.dot(normed, w_qkv[...], preferred_element_type=F32)
     high = partial.astype(BF16)
@@ -177,12 +187,12 @@
 
     row_of_lane = lax.broadcasted_iota(jnp.int32, (KV * 8, HD), 1)
     row_number = (row_of_lane % ROWS).astype(F32)
+    everyone = first_all[...].reshape(KV * 8, HD)
     sub3 = lax.broadcasted_iota(jnp.int32, (KV, 8, HD), 1)
     sends = (send0, send1, send2)
     recvs = (recv0, recv1, recv2)
     for c, (start, count, rows) in enumerate(CHUNKS):
-        owners = first_all[:, 8 + 8 * c : 16 + 8 * c, :].reshape(KV * 8, HD)
-        hit = jnp.where(owners == row_number, 1.0, 0.0)
+        hit = jnp.where(everyone[:, c : c + 1] == row_number, 1.0, 0.0)
         pick = jnp.concatenate([hit, jnp.where(row_of_lane < ROWS, hit, 0.0)], axis=1).astype(BF16)
         packed = jnp.dot(pick, stacked, preferred_element_type=F32).reshape(KV, 8, ENTRIES * HD)
         per_tile = 8 // count
@@ -239,10 +249,6 @@
             top = jnp.max(scores, axis=1, keepdims=True)
             weights = jnp.exp(scores - top)
             block_total = jnp.sum(weights, axis=1, keepdims=True)
-            values = jnp.concatenate([v_v[a], v_v[b]], axis=1)
-            both = jnp.dot(weights.astype(BF16), values, preferred_element_type=F32)
-            block_out = jnp.where(sub16 < 8, both[:, :HD], both[:, HD:])
-
             is_first = jnp.where(column < 8, table[1, a], table[1, b]) == 0
             own = jnp.sum(queries * new_keys, axis=1, keepdims=True) * SCALE
             own = jnp.where(is_first, own, FLOOR)
@@ -250,17 +256,21 @@
             factor = jnp.exp(top - highest)
             own_weight = jnp.where(is_first, jnp.exp(own - highest), 0.0)
             slot_total = block_total * factor + own_weight
-            slot_out = (block_out * factor + own_weight * new_values) / slot_total
-            outs_all[PEERS, 16 * pair : 16 * pair + 16, :] = slot_out.astype(BF16)
             for s, part in ((a, slice(0, 8)), (b, slice(8, 16))):
                 stats = jnp.where(lane == s, highest[part], stats)
                 stats = jnp.where(lane == 16 + s, slot_total[part], stats)
+            if b == SLOTS - 1:
+                stats_all[PEERS] = stats
+                for j, offset in enumerate(OFFSETS):
+                    send(7, stats_all.at[PEERS], stats_all.at[j], ahead(offset))
+            values = jnp.concatenate([v_v[a], v_v[b]], axis=1)
+            both = jnp.dot(weights.astype(BF16), values, preferred_element_type=F32)
+            block_out = jnp.where(sub16 < 8, both[:, :HD], both[:, HD:])
+            slot_out = (block_out * factor + own_weight * new_values) / slot_total
+            outs_all[PEERS, 16 * pair : 16 * pair + 16, :] = slot_out.astype(BF16)
         part = pl.ds(8 * start, 8 * count)
         for j, offset in enumerate(OFFSETS):
             send(4 + c, outs_all.at[PEERS, part], outs_all.at[j, part], ahead(offset))
-    stats_all[PEERS] = stats
-    for j, offset in enumerate(OFFSETS):
-        send(7, stats_all.at[PEERS], stats_all.at[j], ahead(offset))
 
     def side_by_side(tiles, shift):
         near = jnp.full((8, HD), -1.0, F32)
@@ -274,7 +284,7 @@
                 far = jnp.where((lane >= at - HD) & (lane < at + SLOTS - HD), moved, far)
         return jnp.concatenate([near, far], axis=1)
 
-    owners = side_by_side(lambda j: first_all[j, 32:40, :], 0)
+    owners = side_by_side(lambda j: first_all[j], OWNER_LANE)
     belongs = lax.broadcasted_iota(jnp.int32, (ROWS, 2 * HD), 0).astype(F32) == owners[0:1]
 
     wait_bytes(stats_all.at[others], recv_sem.at[7])
@@ -308,11 +318,12 @@
     send(8, half_send, half_recv, sibling)
     own_half = jnp.dot(attended, w_out[:, mine], preferred_element_type=F32)
     wait_bytes(half_recv, recv_sem.at[8])
-    z_all[my_z] = own_half + half_recv[...]
+    z_all[my_z] = (own_half + half_recv[...]).astype(BF16)
     for peer in z_peers:
         send(9, z_all.at[my_z], z_all.at[my_z], peer)
     wait_bytes(z_all.at[pl.ds(0, SIDE - 1)], recv_sem.at[9])
-    done = (((z_all[0] + z_all[1]) + z_all[2]) + z_all[3]).astype(BF16)
+    parts = [z_all[z].astype(F32) for z in range(SIDE)]
+    done = (((parts[0] + parts[1]) + parts[2]) + parts[3]).astype(BF16)
     done_send[...] = done
     send(10, done_send, done_recv, sibling)
     out_ref[:, mine] = done
@@ -332,11 +343,10 @@
 def per_device(tokens, gain, w_qkv, w_out, k_cache, v_cache, lengths, block_table):
     features = tokens.shape[1]
     anywhere = pl.BlockSpec(memory_space=pl.ANY)
-    scalars = pl.BlockSpec(memory_space=pltpu.SMEM)
     return pl.pallas_call(
         kernel,
         out_shape=jax.ShapeDtypeStruct((ROWS, features), BF16),
-        in_specs=[anywhere] * 6 + [scalars] * 2,
+        in_specs=[anywhere] * 8,
         out_specs=pl.BlockSpec(memory_space=pltpu.VMEM),
         scratch_shapes=[
             pltpu.VMEM((ROWS, features), BF16),
@@ -345,7 +355,7 @@
             pltpu.VMEM((G * HD, features), BF16),
             pltpu.VMEM((SLOTS, BLK, HD), BF16),
             pltpu.VMEM((SLOTS, BLK, HD), BF16),
-            pltpu.VMEM((KV, 40, HD), F32),
+            pltpu.VMEM((KV, 8, HD), F32),
         ]
         + [pltpu.VMEM((KV, rows, HD), F32) for _, _, rows in CHUNKS]
         + [pltpu.VMEM((PEERS, rows, HD), F32) for _, _, rows in CHUNKS]
@@ -356,10 +366,12 @@
             pltpu.VMEM((KV * SLOTS * G, HD), F32),
             pltpu.VMEM((ROWS, HALF), F32),
             pltpu.VMEM((ROWS, HALF), F32),
-            pltpu.VMEM((SIDE, ROWS, HALF), F32),
+            pltpu.VMEM((SIDE, ROWS, HALF), BF16),
             pltpu.VMEM((ROWS, HALF), BF16),
             pltpu.VMEM((ROWS, HALF), BF16),
-            pltpu.SemaphoreType.DMA((4,)),
+            pltpu.SMEM((ROWS,), jnp.int32),
+            pltpu.SMEM((2, SLOTS), jnp.int32),
+            pltpu.SemaphoreType.DMA((6,)),
             pltpu.SemaphoreType.DMA((2, SLOTS // 2)),
             pltpu.SemaphoreType.DMA((11,)),
             pltpu.SemaphoreType.DMA((11,)),

time: 49.7 us -> 42.7 us (0.86)
  Pallas kernels: 48 us -> 41 us
    pallas_call x1, Pallas kernels: 48 us -> 41 us  [per_device(): pl.pallas_call(kernel, out_shape=jax.ShapeDtypeStruct((ROWS, features), B...]
where the time goes in v2:
time: 42.7 us; the launch traced here: 42.5 us
  Pallas kernels  41 us (96%)
  local copies, waits for them, and re-layouts  1.47 us (3%)
    pallas_call x1, Pallas kernels, per_device(): pl.pallas_call(kernel, out_shape=jax.ShapeDtypeStruct((ROWS, features), B...  41 us
    unnamed x1, local copies, waits for them, and re-layouts  1.47 us

profile of v2, /device:TPU:1, one launch (start us, length us, event | category | flops | bytes accessed | tf_op | source)
XLA Modules:
  0.0 42.5 jit_solution(17338429247709683920)
XLA Ops:
  0.0 41.0 %shard_map.82 = bf16[64,512]{1,0:T(8,128)(2,1)} custom-call(bf16[64,512]{1,0:T(8,128)(2,1)} %tokens_hbm.1, f32[1,512]{1,0:T(1,128)} %bitcast.10, bf16[512,1280]{1,0:T(8,128)(2,1)} %bitcast.8, bf16[1024,512]{1,0:T(8,128)(2,1)} %bitcast.9, bf16[10,4096,128]{2,1,0:T(8,128)(2,1)} %bitcast.6, bf16[10,4096,128]{2,1,0:T(8,128)(2,1)} %bitcast.7, s32[64]{0:T(128)} %lengths_hbm.1, ...), custom_call_target="tpu_custom_call" | custom-call | tf_op jit(solution)/shard_map/pallas_call | solution.py:346
  41.1 1.5 %copy.10 = bf16[64,512]{1,0:T(8,128)(2,1)} copy(bf16[64,512]{1,0:T(8,128)(2,1)} %shard_map.82) | data formatting | bytes 131072

commit v3 on v2

--- a/solution.py
+++ b/solution.py
@@ -26,13 +26,18 @@
 MESH = pl.DeviceIdType.MESH
 F32 = jnp.float32
 BF16 = jnp.bfloat16
-NT = (((1,), (1,)), ((), ()))
 
 SQUARE_LANE = 8
 OWNER_LANE = 16
 
-EARLY_PAIRS = 3
-CHUNKS = ((0, 4, 40), (4, 4, 40), (8, 2, 24))
+EARLY_VALUES = 1
+EARLY_KEYS = 3
+TURN = 512
+
+CHUNKS = ((0, 2, 32), (2, 4, 48), (6, 4, 48))
+LANES = (128, 0, 64)
+
+STEPS = 32000.0
 
 
 def ring_distance(step):
@@ -64,6 +69,7 @@
     w_qkv,
     w_out,
     k_v,
+    k_turned,
     v_v,
     first_all,
     send0,
@@ -73,14 +79,17 @@
     recv1,
     recv2,
     query_rows,
-    outs_all,
+    outs0,
+    outs1,
+    outs2,
     stats_all,
-    outs_wide,
+    wide0,
+    wide1,
+    wide2,
     half_send,
     half_recv,
     z_all,
     done_send,
-    done_recv,
     lengths,
     table,
     load_sem,
@@ -123,8 +132,9 @@
         v_loads.append(pltpu.make_async_copy(v_hbm.at[part], v_v.at[part], kv_sem.at[1, pair]))
     for load in loads[:3] + loads[4:]:
         load.start()
-    for pair in range(EARLY_PAIRS):
+    for pair in range(SLOTS // 2):
         k_loads[pair].start()
+    for pair in range(EARLY_VALUES):
         v_loads[pair].start()
 
     sub = lax.broadcasted_iota(jnp.int32, (8, HD), 0)
@@ -162,12 +172,22 @@
 
     for j, offset in enumerate(OFFSETS):
         send(0, first_all.at[PEERS], first_all.at[j], ahead(offset))
+
+    def turn_keys(pair):
+        k_loads[pair].wait()
+        for half in range(2):
+            for at in range(0, BLK, TURN):
+                k_turned[pair, HD * half : HD * half + HD, at : at + TURN] = k_v[
+                    2 * pair + half, at : at + TURN
+                ].T
+
+    for pair in range(EARLY_KEYS):
+        turn_keys(pair)
     loads[1].wait()
     loads[2].wait()
     wait_bytes(first_all.at[others], recv_sem.at[0])
 
-    for pair in range(EARLY_PAIRS, SLOTS // 2):
-        k_loads[pair].start()
+    for pair in range(EARLY_VALUES, SLOTS // 2):
         v_loads[pair].start()
     loads[3].start()
     squares = first_all[0]
@@ -179,24 +199,35 @@
         [tokens[8 * k : 8 * k + 8] * inverse[:, SQUARE_LANE + k : SQUARE_LANE + k + 1] * gains for k in range(ROWS // 8)], axis=0
     ).astype(BF16)
     partial = jnp.dot(normed, w_qkv[...], preferred_element_type=F32)
-    high = partial.astype(BF16)
-    rest = partial - high.astype(F32)
-    middle = rest.astype(BF16)
-    low = (rest - middle.astype(F32)).astype(BF16)
-    stacked = jnp.concatenate([high, middle, low, jnp.zeros_like(low)], axis=0)
+    largest = jnp.max(jnp.abs(partial), axis=1, keepdims=True)
+    exponent = jnp.ceil(jnp.log2(jnp.maximum(largest, 1e-30)))
+    whole = jnp.round(partial * (STEPS * jnp.exp2(-exponent)))
+    coarse = jnp.floor(whole * (1.0 / 256.0))
+    fine = whole - 256.0 * coarse
+    exponents = jnp.broadcast_to(exponent, (ROWS, HD))
+    stacked = jnp.concatenate(
+        [
+            jnp.concatenate([coarse, jnp.zeros_like(exponents)], axis=1),
+            jnp.concatenate([fine, exponents], axis=1),
+        ],
+        axis=0,
+    ).astype(BF16)
 
     row_of_lane = lax.broadcasted_iota(jnp.int32, (KV * 8, HD), 1)
     row_number = (row_of_lane % ROWS).astype(F32)
+    part_weight = jnp.where(row_of_lane < ROWS, 256.0, 1.0)
     everyone = first_all[...].reshape(KV * 8, HD)
     sub3 = lax.broadcasted_iota(jnp.int32, (KV, 8, HD), 1)
     sends = (send0, send1, send2)
     recvs = (recv0, recv1, recv2)
+    outs = (outs0, outs1, outs2)
+    wides = (wide0, wide1, wide2)
     for c, (start, count, rows) in enumerate(CHUNKS):
-        hit = jnp.where(everyone[:, c : c + 1] == row_number, 1.0, 0.0)
-        pick = jnp.concatenate([hit, jnp.where(row_of_lane < ROWS, hit, 0.0)], axis=1).astype(BF16)
-        packed = jnp.dot(pick, stacked, preferred_element_type=F32).reshape(KV, 8, ENTRIES * HD)
+        pick = jnp.where(everyone[:, c : c + 1] == row_number, part_weight, 0.0).astype(BF16)
+        packed = jnp.dot(pick, stacked, preferred_element_type=F32).reshape(KV, 8, (ENTRIES + 1) * HD)
         per_tile = 8 // count
-        for k in range(rows // 8):
+        tiles = []
+        for k in range(rows // 8 - 1):
             tile = packed[:, :, per_tile * k * HD : (per_tile * k + 1) * HD]
             for e in range(1, per_tile):
                 entry = per_tile * k + e
@@ -204,9 +235,14 @@
                     tile = jnp.where(
                         sub3 >= e * count, packed[:, :, entry * HD : (entry + 1) * HD], tile
                     )
-            sends[c][:, 8 * k : 8 * k + 8, :] = tile
+            tiles.append(tile)
+        tiles.append(packed[:, :, ENTRIES * HD :])
+        sends[c][...] = jnp.concatenate(tiles, axis=1).astype(jnp.int32).astype(jnp.int16)
         for j, offset in enumerate(OFFSETS):
             send(1 + c, sends[c].at[j], recvs[c].at[j], behind(offset))
+
+    for pair in range(EARLY_KEYS, SLOTS // 2):
+        turn_keys(pair)
 
     sub16 = lax.broadcasted_iota(jnp.int32, (16, HD), 0)
     column = lax.broadcasted_iota(jnp.int32, (16, 1), 0)
@@ -215,9 +251,12 @@
 
     for c, (start, count, rows) in enumerate(CHUNKS):
         wait_bytes(recvs[c].at[others], recv_sem.at[1 + c])
-        total = sends[c][PEERS]
-        for j in range(PEERS):
-            total = total + recvs[c][j]
+        total = 0.0
+        for j in range(KV):
+            got = (sends[c][PEERS] if j == PEERS else recvs[c][j]).astype(jnp.int32).astype(F32)
+            got = got.reshape(rows // 8, 8, HD)
+            total = total + got[:-1] * (jnp.exp2(got[-1:]) * (1.0 / STEPS))
+        total = total.reshape(rows - 8, HD)
         total = total.astype(BF16).astype(F32)
         per_tile = 8 // count
         for entry in range(ENTRIES):
@@ -226,7 +265,6 @@
 
         for pair in range(start // 2, (start + count) // 2):
             a, b = 2 * pair, 2 * pair + 1
-            k_loads[pair].wait()
             v_loads[pair].wait()
             queries = jnp.concatenate(
                 [query_rows[16 * a : 16 * a + 8, :], query_rows[16 * b : 16 * b + 8, :]], axis=0
@@ -240,8 +278,7 @@
             left = jnp.concatenate(
                 [jnp.where(sub16 < 8, queries, 0.0), jnp.where(sub16 < 8, 0.0, queries)], axis=1
             ).astype(BF16)
-            keys = jnp.concatenate([k_v[a], k_v[b]], axis=1)
-            scores = lax.dot_general(left, keys, NT, preferred_element_type=F32) * SCALE
+            scores = jnp.dot(left, k_turned[pair], preferred_element_type=F32) * SCALE
             limit_a = lengths[jnp.maximum(table[0, a], 0)] - BLK * table[1, a]
             limit_b = lengths[jnp.maximum(table[0, b], 0)] - BLK * table[1, b]
             limit = jnp.where(column < 8, limit_a, limit_b)
@@ -267,22 +304,19 @@
             both = jnp.dot(weights.astype(BF16), values, preferred_element_type=F32)
             block_out = jnp.where(sub16 < 8, both[:, :HD], both[:, HD:])
             slot_out = (block_out * factor + own_weight * new_values) / slot_total
-            outs_all[PEERS, 16 * pair : 16 * pair + 16, :] = slot_out.astype(BF16)
-        part = pl.ds(8 * start, 8 * count)
+            at = 8 * (a - start)
+            outs[c][PEERS, at : at + 16, :] = slot_out.astype(BF16)
         for j, offset in enumerate(OFFSETS):
-            send(4 + c, outs_all.at[PEERS, part], outs_all.at[j, part], ahead(offset))
+            send(4 + c, outs[c].at[PEERS], outs[c].at[j], ahead(offset))
 
     def side_by_side(tiles, shift):
-        near = jnp.full((8, HD), -1.0, F32)
-        far = jnp.full((8, HD), -1.0, F32)
-        for j in range(KV):
-            at = SLOTS * j
-            moved = pltpu.roll(tiles(j), (at - shift) % HD, 1)
-            if at < HD:
-                near = jnp.where((lane >= at) & (lane < at + SLOTS), moved, near)
-            if at + SLOTS > HD:
-                far = jnp.where((lane >= at - HD) & (lane < at + SLOTS - HD), moved, far)
-        return jnp.concatenate([near, far], axis=1)
+        halves = [jnp.full((8, HD), -1.0, F32), jnp.full((8, HD), -1.0, F32)]
+        for (start, count, _), first in zip(CHUNKS, LANES):
+            for j in range(KV):
+                half, at = divmod(first + count * j, HD)
+                moved = pltpu.roll(tiles(j), (at - start - shift) % HD, 1)
+                halves[half] = jnp.where((lane >= at) & (lane < at + count), moved, halves[half])
+        return jnp.concatenate(halves, axis=1)
 
     owners = side_by_side(lambda j: first_all[j], OWNER_LANE)
     belongs = lax.broadcasted_iota(jnp.int32, (ROWS, 2 * HD), 0).astype(F32) == owners[0:1]
@@ -300,13 +334,19 @@
         lower = (share - upper.astype(F32)).astype(BF16)
         shares.append(jnp.concatenate([upper, lower], axis=0))
 
-    for c, (start, count, rows) in enumerate(CHUNKS):
-        wait_bytes(outs_all.at[others, pl.ds(8 * start, 8 * count)], recv_sem.at[4 + c])
-    outs_wide[...] = outs_all[...].astype(F32).reshape(KV * SLOTS * G, HD)
+    def arrived(c):
+        wait_bytes(outs[c].at[others], recv_sem.at[4 + c])
+        wides[c][...] = outs[c][...].astype(F32).reshape(wides[c].shape)
+
+    def slots_of(c, g):
+        return wides[c][pl.ds(g, wides[c].shape[0] // G, stride=G), :].astype(BF16)
+
+    for c in range(len(CHUNKS)):
+        arrived(c)
     attended = []
     for g in range(G):
-        slots = outs_wide[pl.ds(g, KV * SLOTS, stride=G), :].astype(BF16)
-        slots = jnp.concatenate([slots, jnp.zeros((2 * HD - KV * SLOTS, HD), BF16)], axis=0)
+        slots = [slots_of(c, g) for c in sorted(range(len(CHUNKS)), key=lambda c: LANES[c])]
+        slots = jnp.concatenate(slots + [jnp.zeros((2 * HD - KV * SLOTS, HD), BF16)], axis=0)
         both = jnp.dot(shares[g], slots, preferred_element_type=F32)
         attended.append((both[:ROWS] + both[ROWS:]).astype(BF16))
     attended = jnp.concatenate(attended, axis=1)
@@ -325,19 +365,20 @@
     parts = [z_all[z].astype(F32) for z in range(SIDE)]
     done = (((parts[0] + parts[1]) + parts[2]) + parts[3]).astype(BF16)
     done_send[...] = done
-    send(10, done_send, done_recv, sibling)
-    out_ref[:, mine] = done
-    wait_bytes(done_recv, recv_sem.at[10])
-    out_ref[:, theirs] = done_recv[...]
+    send(10, done_send, out_ref.at[:, mine], sibling)
+    keep = pltpu.make_async_copy(done_send, out_ref.at[:, mine], load_sem.at[6])
+    keep.start()
 
     wait_bytes(first_all.at[others], send_sem.at[0])
     for c, (start, count, rows) in enumerate(CHUNKS):
         wait_bytes(sends[c].at[others], send_sem.at[1 + c])
-        wait_bytes(outs_all.at[others, pl.ds(8 * start, 8 * count)], send_sem.at[4 + c])
+        wait_bytes(outs[c].at[others], send_sem.at[4 + c])
     wait_bytes(stats_all.at[others], send_sem.at[7])
     wait_bytes(half_send, send_sem.at[8])
     wait_bytes(z_all.at[pl.ds(0, SIDE - 1)], send_sem.at[9])
     wait_bytes(done_send, send_sem.at[10])
+    wait_bytes(out_ref.at[:, theirs], recv_sem.at[10])
+    keep.wait()
 
 
 def per_device(tokens, gain, w_qkv, w_out, k_cache, v_cache, lengths, block_table):
@@ -347,31 +388,33 @@
         kernel,
         out_shape=jax.ShapeDtypeStruct((ROWS, features), BF16),
         in_specs=[anywhere] * 8,
-        out_specs=pl.BlockSpec(memory_space=pltpu.VMEM),
+        out_specs=anywhere,
         scratch_shapes=[
             pltpu.VMEM((ROWS, features), BF16),
             pltpu.VMEM((1, features), F32),
             pltpu.VMEM((features, ENTRIES * HD), BF16),
             pltpu.VMEM((G * HD, features), BF16),
             pltpu.VMEM((SLOTS, BLK, HD), BF16),
+            pltpu.VMEM((SLOTS // 2, 2 * HD, BLK), BF16),
             pltpu.VMEM((SLOTS, BLK, HD), BF16),
             pltpu.VMEM((KV, 8, HD), F32),
         ]
-        + [pltpu.VMEM((KV, rows, HD), F32) for _, _, rows in CHUNKS]
-        + [pltpu.VMEM((PEERS, rows, HD), F32) for _, _, rows in CHUNKS]
+        + [pltpu.VMEM((KV, rows, HD), jnp.int16) for _, _, rows in CHUNKS]
+        + [pltpu.VMEM((PEERS, rows, HD), jnp.int16) for _, _, rows in CHUNKS]
         + [
             pltpu.VMEM((SLOTS * 16, HD), F32),
-            pltpu.VMEM((KV, SLOTS * G, HD), BF16),
-            pltpu.VMEM((KV, 8, HD), F32),
-            pltpu.VMEM((KV * SLOTS * G, HD), F32),
+        ]
+        + [pltpu.VMEM((KV, count * G, HD), BF16) for _, count, _ in CHUNKS]
+        + [pltpu.VMEM((KV, 8, HD), F32)]
+        + [pltpu.VMEM((KV * count * G, HD), F32) for _, count, _ in CHUNKS]
+        + [
             pltpu.VMEM((ROWS, HALF), F32),
             pltpu.VMEM((ROWS, HALF), F32),
             pltpu.VMEM((SIDE, ROWS, HALF), BF16),
             pltpu.VMEM((ROWS, HALF), BF16),
-            pltpu.VMEM((ROWS, HALF), BF16),
             pltpu.SMEM((ROWS,), jnp.int32),
             pltpu.SMEM((2, SLOTS), jnp.int32),
-            pltpu.SemaphoreType.DMA((6,)),
+            pltpu.SemaphoreType.DMA((7,)),
             pltpu.SemaphoreType.DMA((2, SLOTS // 2)),
             pltpu.SemaphoreType.DMA((11,)),
             pltpu.SemaphoreType.DMA((11,)),

time: 42.7 us -> 39.3 us (0.920)
  Pallas kernels: 41 us -> 37.7 us
    pallas_call x1, Pallas kernels: 41 us -> 37.7 us  [per_device(): pl.pallas_call(kernel, out_shape=jax.ShapeDtypeStruct((ROWS, features), B...]
where the time goes in v3:
time: 39.3 us; the launch traced here: 39.2 us
  Pallas kernels  37.7 us (96%)
  local copies, waits for them, and re-layouts  1.47 us (4%)
    pallas_call x1, Pallas kernels, per_device(): pl.pallas_call(kernel, out_shape=jax.ShapeDtypeStruct((ROWS, features), B...  37.7 us
    unnamed x1, local copies, waits for them, and re-layouts  1.47 us

profile of v3, /device:TPU:1, one launch (start us, length us, event | category | flops | bytes accessed | tf_op | source)
XLA Modules:
  0.0 39.2 jit_solution(10151459169061582323)
XLA Ops:
  0.0 37.7 %shard_map.82 = bf16[64,512]{1,0:T(8,128)(2,1)} custom-call(bf16[64,512]{1,0:T(8,128)(2,1)} %tokens_hbm.1, f32[1,512]{1,0:T(1,128)} %bitcast.10, bf16[512,1280]{1,0:T(8,128)(2,1)} %bitcast.8, bf16[1024,512]{1,0:T(8,128)(2,1)} %bitcast.9, bf16[10,4096,128]{2,1,0:T(8,128)(2,1)} %bitcast.6, bf16[10,4096,128]{2,1,0:T(8,128)(2,1)} %bitcast.7, s32[64]{0:T(128)} %lengths_hbm.1, ...), custom_call_target="tpu_custom_call" | custom-call | tf_op jit(solution)/shard_map/pallas_call | solution.py:387
  37.7 1.5 %copy.10 = bf16[64,512]{1,0:T(8,128)(2,1)} copy(bf16[64,512]{1,0:T(8,128)(2,1)} %shard_map.82) | data formatting | bytes 131072

commit v4 on v3

--- a/solution.py
+++ b/solution.py
@@ -34,8 +34,8 @@
 EARLY_KEYS = 3
 TURN = 512
 
-CHUNKS = ((0, 2, 32), (2, 4, 48), (6, 4, 48))
-LANES = (128, 0, 64)
+CHUNKS = ((0, 4, 48), (4, 4, 48), (8, 2, 32))
+LANES = (0, 64, 128)
 
 STEPS = 32000.0
 
@@ -249,6 +249,45 @@
     position = lax.broadcasted_iota(jnp.int32, (16, BLK), 1)
     stats = jnp.zeros((8, HD), F32)
 
+    def of_pair(pair, entry):
+        a, b = 32 * pair + entry, 32 * pair + 16 + entry
+        return jnp.where(sub16 < 8, query_rows[a : a + 1, :], query_rows[b : b + 1, :])
+
+    def score(pair):
+        a, b = 32 * pair, 32 * pair + 16
+        queries = jnp.concatenate([query_rows[a : a + G, :], query_rows[b : b + G, :]], axis=0)
+        left = jnp.concatenate(
+            [jnp.where(sub16 < 8, queries, 0.0), jnp.where(sub16 < 8, 0.0, queries)], axis=1
+        ).astype(BF16)
+        return queries, jnp.dot(left, k_turned[pair], preferred_element_type=F32)
+
+    def soften(pair, queries, scores):
+        a, b = 2 * pair, 2 * pair + 1
+        limit_a = lengths[jnp.maximum(table[0, a], 0)] - BLK * table[1, a]
+        limit_b = lengths[jnp.maximum(table[0, b], 0)] - BLK * table[1, b]
+        limit = jnp.where(column < 8, limit_a, limit_b)
+        scores = jnp.where(position < limit, scores * SCALE, FLOOR)
+        top = jnp.max(scores, axis=1, keepdims=True)
+        weights = jnp.exp(scores - top)
+        block_total = jnp.sum(weights, axis=1, keepdims=True)
+        is_first = jnp.where(column < 8, table[1, a], table[1, b]) == 0
+        own = jnp.sum(queries * of_pair(pair, G), axis=1, keepdims=True) * SCALE
+        own = jnp.where(is_first, own, FLOOR)
+        highest = jnp.maximum(top, own)
+        factor = jnp.exp(top - highest)
+        own_weight = jnp.where(is_first, jnp.exp(own - highest), 0.0)
+        slot_total = block_total * factor + own_weight
+        return highest, slot_total, factor, own_weight, weights.astype(BF16)
+
+    def weigh(pair, highest, slot_total, factor, own_weight, weights):
+        values = jnp.concatenate([v_v[2 * pair], v_v[2 * pair + 1]], axis=1)
+        both = jnp.dot(weights, values, preferred_element_type=F32)
+        block_out = jnp.where(sub16 < 8, both[:, :HD], both[:, HD:])
+        slot_out = (block_out * factor + own_weight * of_pair(pair, G + 1)) / slot_total
+        return slot_out.astype(BF16)
+
+    for load in v_loads:
+        load.wait()
     for c, (start, count, rows) in enumerate(CHUNKS):
         wait_bytes(recvs[c].at[others], recv_sem.at[1 + c])
         total = 0.0
@@ -263,49 +302,24 @@
             row = entry * count
             query_rows[pl.ds(16 * start + entry, count, stride=16), :] = total[row : row + count]
 
-        for pair in range(start // 2, (start + count) // 2):
-            a, b = 2 * pair, 2 * pair + 1
-            v_loads[pair].wait()
-            queries = jnp.concatenate(
-                [query_rows[16 * a : 16 * a + 8, :], query_rows[16 * b : 16 * b + 8, :]], axis=0
-            )
-            new_keys = jnp.where(
-                sub16 < 8, query_rows[16 * a + 8 : 16 * a + 9, :], query_rows[16 * b + 8 : 16 * b + 9, :]
-            )
-            new_values = jnp.where(
-                sub16 < 8, query_rows[16 * a + 9 : 16 * a + 10, :], query_rows[16 * b + 9 : 16 * b + 10, :]
-            )
-            left = jnp.concatenate(
-                [jnp.where(sub16 < 8, queries, 0.0), jnp.where(sub16 < 8, 0.0, queries)], axis=1
-            ).astype(BF16)
-            scores = jnp.dot(left, k_turned[pair], preferred_element_type=F32) * SCALE
-            limit_a = lengths[jnp.maximum(table[0, a], 0)] - BLK * table[1, a]
-            limit_b = lengths[jnp.maximum(table[0, b], 0)] - BLK * table[1, b]
-            limit = jnp.where(column < 8, limit_a, limit_b)
-            scores = jnp.where(position < limit, scores, FLOOR)
-            top = jnp.max(scores, axis=1, keepdims=True)
-            weights = jnp.exp(scores - top)
-            block_total = jnp.sum(weights, axis=1, keepdims=True)
-            is_first = jnp.where(column < 8, table[1, a], table[1, b]) == 0
-            own = jnp.sum(queries * new_keys, axis=1, keepdims=True) * SCALE
-            own = jnp.where(is_first, own, FLOOR)
-            highest = jnp.maximum(top, own)
-            factor = jnp.exp(top - highest)
-            own_weight = jnp.where(is_first, jnp.exp(own - highest), 0.0)
-            slot_total = block_total * factor + own_weight
-            for s, part in ((a, slice(0, 8)), (b, slice(8, 16))):
+        pairs = range(start // 2, (start + count) // 2)
+        ready = {}
+        for pair in pairs:
+            queries, scores = score(pair)
+            ready[pair] = (queries, scores)
+        for pair in pairs:
+            ready[pair] = soften(pair, *ready[pair])
+            highest, slot_total = ready[pair][:2]
+            for s, part in ((2 * pair, slice(0, 8)), (2 * pair + 1, slice(8, 16))):
                 stats = jnp.where(lane == s, highest[part], stats)
                 stats = jnp.where(lane == 16 + s, slot_total[part], stats)
-            if b == SLOTS - 1:
-                stats_all[PEERS] = stats
-                for j, offset in enumerate(OFFSETS):
-                    send(7, stats_all.at[PEERS], stats_all.at[j], ahead(offset))
-            values = jnp.concatenate([v_v[a], v_v[b]], axis=1)
-            both = jnp.dot(weights.astype(BF16), values, preferred_element_type=F32)
-            block_out = jnp.where(sub16 < 8, both[:, :HD], both[:, HD:])
-            slot_out = (block_out * factor + own_weight * new_values) / slot_total
-            at = 8 * (a - start)
-            outs[c][PEERS, at : at + 16, :] = slot_out.astype(BF16)
+        if start + count == SLOTS:
+            stats_all[PEERS] = stats
+            for j, offset in enumerate(OFFSETS):
+                send(7, stats_all.at[PEERS], stats_all.at[j], ahead(offset))
+        for pair in pairs:
+            at = 16 * pair - 8 * start
+            outs[c][PEERS, at : at + 16, :] = weigh(pair, *ready[pair])
         for j, offset in enumerate(OFFSETS):
             send(4 + c, outs[c].at[PEERS], outs[c].at[j], ahead(offset))
 
@@ -328,8 +342,7 @@
     for g in range(G):
         masked = jnp.where(belongs, tops[g : g + 1], -3e38)
         highest = jnp.max(masked, axis=1, keepdims=True)
-        share = jnp.where(belongs, jnp.exp(masked - highest) * totals[g : g + 1], 0.0)
-        share = share / jnp.sum(share, axis=1, keepdims=True)
+        share = jnp.exp(masked - highest) * totals[g : g + 1]
         upper = share.astype(BF16)
         lower = (share - upper.astype(F32)).astype(BF16)
         shares.append(jnp.concatenate([upper, lower], axis=0))
@@ -343,12 +356,16 @@
 
     for c in range(len(CHUNKS)):
         arrived(c)
+    ones = jnp.ones((2 * HD, HD), BF16)
     attended = []
     for g in range(G):
         slots = [slots_of(c, g) for c in sorted(range(len(CHUNKS)), key=lambda c: LANES[c])]
         slots = jnp.concatenate(slots + [jnp.zeros((2 * HD - KV * SLOTS, HD), BF16)], axis=0)
-        both = jnp.dot(shares[g], slots, preferred_element_type=F32)
-        attended.append((both[:ROWS] + both[ROWS:]).astype(BF16))
+        both = jnp.dot(
+            shares[g], jnp.concatenate([slots, ones], axis=1), preferred_element_type=F32
+        )
+        both = both[:ROWS] + both[ROWS:]
+        attended.append((both[:, :HD] / both[:, HD:]).astype(BF16))
     attended = jnp.concatenate(attended, axis=1)
 
     loads[3].wait()
@@ -386,9 +403,9 @@
     anywhere = pl.BlockSpec(memory_space=pl.ANY)
     return pl.pallas_call(
         kernel,
-        out_shape=jax.ShapeDtypeStruct((ROWS, features), BF16),
+        out_shape=pltpu.VMEM((ROWS, features), BF16),
         in_specs=[anywhere] * 8,
-        out_specs=anywhere,
+        out_specs=pl.BlockSpec(memory_space=pltpu.VMEM),
         scratch_shapes=[
             pltpu.VMEM((ROWS, features), BF16),
             pltpu.VMEM((1, features), F32),

time: 39.3 us -> 35.7 us (0.908)
  Pallas kernels: 37.7 us -> 34.9 us
  local copies, waits for them, and re-layouts: 1.47 us -> 0.63 us
    pallas_call x1, Pallas kernels: 37.7 us -> 34.9 us  [per_device(): pl.pallas_call(kernel, out_shape=pltpu.VMEM((ROWS, features), BF16), in_s...]
    unnamed x1, local copies, waits for them, and re-layouts: 1.47 us -> 0.63 us
where the time goes in v4:
time: 35.7 us; the launch traced here: 35.6 us
  Pallas kernels  34.9 us (98%)
  local copies, waits for them, and re-layouts  0.63 us (2%)
    pallas_call x1, Pallas kernels, per_device(): pl.pallas_call(kernel, out_shape=pltpu.VMEM((ROWS, features), BF16), in_s...  34.9 us

profile of v4, /device:TPU:1, one launch (start us, length us, event | category | flops | bytes accessed | tf_op | source)
XLA Modules:
  0.0 35.6 jit_solution(13307073824674717775)
XLA Ops:
  0.0 34.9 %shard_map.82 = bf16[64,512]{1,0:T(8,128)(2,1)S(1)} custom-call(bf16[64,512]{1,0:T(8,128)(2,1)} %tokens_hbm.1, f32[1,512]{1,0:T(1,128)} %bitcast.10, bf16[512,1280]{1,0:T(8,128)(2,1)} %bitcast.8, bf16[1024,512]{1,0:T(8,128)(2,1)} %bitcast.9, bf16[10,4096,128]{2,1,0:T(8,128)(2,1)} %bitcast.6, bf16[10,4096,128]{2,1,0:T(8,128)(2,1)} %bitcast.7, s32[64]{0:T(128)} %lengths_hbm.1, ...), custom_call_target="tpu_custom_call" | custom-call | tf_op jit(solution)/shard_map/pallas_call | solution.py:404
  35.0 0.6 %copy.10 = bf16[64,512]{1,0:T(8,128)(2,1)} copy(bf16[64,512]{1,0:T(8,128)(2,1)S(1)} %shard_map.82) | data formatting | bytes 131072

commit v5 on v4

--- a/solution.py
+++ b/solution.py
@@ -34,8 +34,10 @@
 EARLY_KEYS = 3
 TURN = 512
 
-CHUNKS = ((0, 4, 48), (4, 4, 48), (8, 2, 32))
+CHUNKS = ((0, 4, 48), (4, 4, 48), (8, 2, 16))
 LANES = (0, 64, 128)
+TOP_LANES = (0, 64, 32)
+TOTAL_LANES = (16, 80, 96)
 
 STEPS = 32000.0
 
@@ -204,14 +206,9 @@
     whole = jnp.round(partial * (STEPS * jnp.exp2(-exponent)))
     coarse = jnp.floor(whole * (1.0 / 256.0))
     fine = whole - 256.0 * coarse
+    stacked = jnp.concatenate([coarse, fine], axis=0).astype(BF16)
     exponents = jnp.broadcast_to(exponent, (ROWS, HD))
-    stacked = jnp.concatenate(
-        [
-            jnp.concatenate([coarse, jnp.zeros_like(exponents)], axis=1),
-            jnp.concatenate([fine, exponents], axis=1),
-        ],
-        axis=0,
-    ).astype(BF16)
+    exponents = jnp.concatenate([jnp.zeros_like(exponents), exponents], axis=0).astype(BF16)
 
     row_of_lane = lax.broadcasted_iota(jnp.int32, (KV * 8, HD), 1)
     row_number = (row_of_lane % ROWS).astype(F32)
@@ -222,24 +219,39 @@
     recvs = (recv0, recv1, recv2)
     outs = (outs0, outs1, outs2)
     wides = (wide0, wide1, wide2)
-    for c, (start, count, rows) in enumerate(CHUNKS):
-        pick = jnp.where(everyone[:, c : c + 1] == row_number, part_weight, 0.0).astype(BF16)
-        packed = jnp.dot(pick, stacked, preferred_element_type=F32).reshape(KV, 8, (ENTRIES + 1) * HD)
+    picks = [
+        jnp.where(everyone[:, c : c + 1] == row_number, part_weight, 0.0).astype(BF16)
+        for c in range(len(CHUNKS))
+    ]
+
+    def packed(c):
+        _, count, _ = CHUNKS[c]
+        got = jnp.dot(picks[c], stacked, preferred_element_type=F32).reshape(KV, 8, ENTRIES * HD)
         per_tile = 8 // count
         tiles = []
-        for k in range(rows // 8 - 1):
-            tile = packed[:, :, per_tile * k * HD : (per_tile * k + 1) * HD]
-            for e in range(1, per_tile):
-                entry = per_tile * k + e
-                if entry < ENTRIES:
-                    tile = jnp.where(
-                        sub3 >= e * count, packed[:, :, entry * HD : (entry + 1) * HD], tile
-                    )
+        for first in range(0, ENTRIES, per_tile):
+            tile = got[:, :, first * HD : (first + 1) * HD]
+            for e in range(1, min(per_tile, ENTRIES - first)):
+                tile = jnp.where(
+                    sub3 >= e * count, got[:, :, (first + e) * HD : (first + e + 1) * HD], tile
+                )
             tiles.append(tile)
-        tiles.append(packed[:, :, ENTRIES * HD :])
+        return tiles
+
+    def send_rows(c, tiles):
         sends[c][...] = jnp.concatenate(tiles, axis=1).astype(jnp.int32).astype(jnp.int16)
         for j, offset in enumerate(OFFSETS):
             send(1 + c, sends[c].at[j], recvs[c].at[j], behind(offset))
+
+    lane3 = lax.broadcasted_iota(jnp.int32, (KV, 8, HD), 2)
+    marks = jnp.zeros((KV, 8, HD), F32)
+    for c, pick in enumerate(picks):
+        mark = jnp.dot(pick, exponents, preferred_element_type=F32).reshape(KV, 8, HD)
+        marks = jnp.where(lane3 == c, mark, marks)
+    send_rows(0, packed(0) + [marks])
+    last_tiles = packed(2)
+    send_rows(1, packed(1) + last_tiles[:1])
+    send_rows(2, last_tiles[1:])
 
     for pair in range(EARLY_KEYS, SLOTS // 2):
         turn_keys(pair)
@@ -292,10 +304,22 @@
         wait_bytes(recvs[c].at[others], recv_sem.at[1 + c])
         total = 0.0
         for j in range(KV):
-            got = (sends[c][PEERS] if j == PEERS else recvs[c][j]).astype(jnp.int32).astype(F32)
-            got = got.reshape(rows // 8, 8, HD)
-            total = total + got[:-1] * (jnp.exp2(got[-1:]) * (1.0 / STEPS))
-        total = total.reshape(rows - 8, HD)
+            first, second, third = (
+                sends[i].at[PEERS] if j == PEERS else recvs[i].at[j] for i in range(len(CHUNKS))
+            )
+            scale = jnp.exp2(first[32:48].astype(jnp.int32).astype(F32)[8:, c : c + 1]) * (1.0 / STEPS)
+            if c < 2:
+                got = (first, second)[c][...].astype(jnp.int32).astype(F32)[:40]
+            else:
+                got = jnp.concatenate(
+                    [
+                        second[32:48].astype(jnp.int32).astype(F32)[8:],
+                        third[...].astype(jnp.int32).astype(F32),
+                    ],
+                    axis=0,
+                )
+            total = total + got.reshape(got.shape[0] // 8, 8, HD) * scale
+        total = total.reshape(total.shape[0] * 8, HD)
         total = total.astype(BF16).astype(F32)
         per_tile = 8 // count
         for entry in range(ENTRIES):
@@ -311,8 +335,8 @@
             ready[pair] = soften(pair, *ready[pair])
             highest, slot_total = ready[pair][:2]
             for s, part in ((2 * pair, slice(0, 8)), (2 * pair + 1, slice(8, 16))):
-                stats = jnp.where(lane == s, highest[part], stats)
-                stats = jnp.where(lane == 16 + s, slot_total[part], stats)
+                stats = jnp.where(lane == TOP_LANES[c] + s - start, highest[part], stats)
+                stats = jnp.where(lane == TOTAL_LANES[c] + s - start, slot_total[part], stats)
         if start + count == SLOTS:
             stats_all[PEERS] = stats
             for j, offset in enumerate(OFFSETS):
@@ -336,8 +360,16 @@
     belongs = lax.broadcasted_iota(jnp.int32, (ROWS, 2 * HD), 0).astype(F32) == owners[0:1]
 
     wait_bytes(stats_all.at[others], recv_sem.at[7])
-    tops = side_by_side(lambda j: stats_all[j], 0)
-    totals = side_by_side(lambda j: stats_all[j], 16)
+    def placed(shift, count):
+        tile = jnp.full((8, HD), -1.0, F32)
+        group = (lane % 64) // count
+        for j in range(KV):
+            tile = jnp.where(group == j, pltpu.roll(stats_all[j], (count * j - shift) % HD, 1), tile)
+        return tile
+
+    last = placed(TOP_LANES[2], 2)
+    tops = jnp.concatenate([placed(TOP_LANES[0], 4), last], axis=1)
+    totals = jnp.concatenate([placed(TOTAL_LANES[0], 4), pltpu.roll(last, 64, 1)], axis=1)
     shares = []
     for g in range(G):
         masked = jnp.where(belongs, tops[g : g + 1], -3e38)
@@ -378,24 +410,21 @@
     z_all[my_z] = (own_half + half_recv[...]).astype(BF16)
     for peer in z_peers:
         send(9, z_all.at[my_z], z_all.at[my_z], peer)
-    wait_bytes(z_all.at[pl.ds(0, SIDE - 1)], recv_sem.at[9])
-    parts = [z_all[z].astype(F32) for z in range(SIDE)]
-    done = (((parts[0] + parts[1]) + parts[2]) + parts[3]).astype(BF16)
-    done_send[...] = done
-    send(10, done_send, out_ref.at[:, mine], sibling)
-    keep = pltpu.make_async_copy(done_send, out_ref.at[:, mine], load_sem.at[6])
-    keep.start()
-
     wait_bytes(first_all.at[others], send_sem.at[0])
     for c, (start, count, rows) in enumerate(CHUNKS):
         wait_bytes(sends[c].at[others], send_sem.at[1 + c])
         wait_bytes(outs[c].at[others], send_sem.at[4 + c])
     wait_bytes(stats_all.at[others], send_sem.at[7])
     wait_bytes(half_send, send_sem.at[8])
+    wait_bytes(z_all.at[pl.ds(0, SIDE - 1)], recv_sem.at[9])
+    parts = [z_all[z].astype(F32) for z in range(SIDE)]
+    done = (((parts[0] + parts[1]) + parts[2]) + parts[3]).astype(BF16)
+    done_send[...] = done
+    send(10, done_send, out_ref.at[:, mine], sibling)
+    out_ref[:, mine] = done
     wait_bytes(z_all.at[pl.ds(0, SIDE - 1)], send_sem.at[9])
     wait_bytes(done_send, send_sem.at[10])
     wait_bytes(out_ref.at[:, theirs], recv_sem.at[10])
-    keep.wait()
 
 
 def per_device(tokens, gain, w_qkv, w_out, k_cache, v_cache, lengths, block_table):
@@ -431,7 +460,7 @@
             pltpu.VMEM((ROWS, HALF), BF16),
             pltpu.SMEM((ROWS,), jnp.int32),
             pltpu.SMEM((2, SLOTS), jnp.int32),
-            pltpu.SemaphoreType.DMA((7,)),
+            pltpu.SemaphoreType.DMA((6,)),
             pltpu.SemaphoreType.DMA((2, SLOTS // 2)),
             pltpu.SemaphoreType.DMA((11,)),
             pltpu.SemaphoreType.DMA((11,)),

time: 35.7 us -> 35.6 us (level)
  no operation moved by 1% of the time
where the time goes in v5:
time: 35.6 us; the launch traced here: 35.5 us
  Pallas kernels  34.8 us (98%)
  local copies, waits for them, and re-layouts  0.63 us (2%)
    pallas_call x1, Pallas kernels, per_device(): pl.pallas_call(kernel, out_shape=pltpu.VMEM((ROWS, features), BF16), in_s...  34.8 us

profile of v5, /device:TPU:1, one launch (start us, length us, event | category | flops | bytes accessed | tf_op | source)
XLA Modules:
  0.0 35.5 jit_solution(8711803036982497206)
XLA Ops:
  0.0 34.8 %shard_map.82 = bf16[64,512]{1,0:T(8,128)(2,1)S(1)} custom-call(bf16[64,512]{1,0:T(8,128)(2,1)} %tokens_hbm.1, f32[1,512]{1,0:T(1,128)} %bitcast.10, bf16[512,1280]{1,0:T(8,128)(2,1)} %bitcast.8, bf16[1024,512]{1,0:T(8,128)(2,1)} %bitcast.9, bf16[10,4096,128]{2,1,0:T(8,128)(2,1)} %bitcast.6, bf16[10,4096,128]{2,1,0:T(8,128)(2,1)} %bitcast.7, s32[64]{0:T(128)} %lengths_hbm.1, ...), custom_call_target="tpu_custom_call" | custom-call | tf_op jit(solution)/shard_map/pallas_call | solution.py:433
  34.8 0.6 %copy.10 = bf16[64,512]{1,0:T(8,128)(2,1)} copy(bf16[64,512]{1,0:T(8,128)(2,1)S(1)} %shard_map.82) | data formatting | bytes 131072

commit v6 on v5

--- a/solution.py
+++ b/solution.py
@@ -448,7 +448,7 @@
         + [pltpu.VMEM((KV, rows, HD), jnp.int16) for _, _, rows in CHUNKS]
         + [pltpu.VMEM((PEERS, rows, HD), jnp.int16) for _, _, rows in CHUNKS]
         + [
-            pltpu.VMEM((SLOTS * 16, HD), F32),
+            pltpu.VMEM((18 * 16, HD), F32),
         ]
         + [pltpu.VMEM((KV, count * G, HD), BF16) for _, count, _ in CHUNKS]
         + [pltpu.VMEM((KV, 8, HD), F32)]

time: 35.6 us -> 35.6 us (level)
  no operation moved by 1% of the time
where the time goes in v6:
time: 35.6 us; the launch traced here: 35.5 us
  Pallas kernels  34.8 us (98%)
  local copies, waits for them, and re-layouts  0.63 us (2%)
    pallas_call x1, Pallas kernels, per_device(): pl.pallas_call(kernel, out_shape=pltpu.VMEM((ROWS, features), BF16), in_s...  34.8 us

profile of v6, /device:TPU:1, one launch (start us, length us, event | category | flops | bytes accessed | tf_op | source)
XLA Modules:
  0.0 35.5 jit_solution(18068017701342164473)
XLA Ops:
  0.0 34.8 %shard_map.82 = bf16[64,512]{1,0:T(8,128)(2,1)S(1)} custom-call(bf16[64,512]{1,0:T(8,128)(2,1)} %tokens_hbm.1, f32[1,512]{1,0:T(1,128)} %bitcast.10, bf16[512,1280]{1,0:T(8,128)(2,1)} %bitcast.8, bf16[1024,512]{1,0:T(8,128)(2,1)} %bitcast.9, bf16[10,4096,128]{2,1,0:T(8,128)(2,1)} %bitcast.6, bf16[10,4096,128]{2,1,0:T(8,128)(2,1)} %bitcast.7, s32[64]{0:T(128)} %lengths_hbm.1, ...), custom_call_target="tpu_custom_call" | custom-call | tf_op jit(solution)/shard_map/pallas_call | solution.py:433
  34.8 0.6 %copy.10 = bf16[64,512]{1,0:T(8,128)(2,1)} copy(bf16[64,512]{1,0:T(8,128)(2,1)S(1)} %shard_map.82) | data formatting | bytes 131072

commit v7 on v6

--- a/solution.py
+++ b/solution.py
@@ -31,7 +31,7 @@
 OWNER_LANE = 16
 
 EARLY_VALUES = 1
-EARLY_KEYS = 3
+EARLY_KEYS = 2
 TURN = 512
 
 CHUNKS = ((0, 4, 48), (4, 4, 48), (8, 2, 16))

time: 35.6 us -> 35.5 us (level)
  no operation moved by 1% of the time
where the time goes in v7:
time: 35.5 us
  Pallas kernels  34.8 us (98%)
  local copies, waits for them, and re-layouts  0.63 us (2%)
    pallas_call x1, Pallas kernels, per_device(): pl.pallas_call(kernel, out_shape=pltpu.VMEM((ROWS, features), BF16), in_s...  34.8 us

profile of v7, /device:TPU:1, one launch (start us, length us, event | category | flops | bytes accessed | tf_op | source)
XLA Modules:
  0.0 35.5 jit_solution(12948193532904627046)
XLA Ops:
  0.0 34.8 %shard_map.82 = bf16[64,512]{1,0:T(8,128)(2,1)S(1)} custom-call(bf16[64,512]{1,0:T(8,128)(2,1)} %tokens_hbm.1, f32[1,512]{1,0:T(1,128)} %bitcast.10, bf16[512,1280]{1,0:T(8,128)(2,1)} %bitcast.8, bf16[1024,512]{1,0:T(8,128)(2,1)} %bitcast.9, bf16[10,4096,128]{2,1,0:T(8,128)(2,1)} %bitcast.6, bf16[10,4096,128]{2,1,0:T(8,128)(2,1)} %bitcast.7, s32[64]{0:T(128)} %lengths_hbm.1, ...), custom_call_target="tpu_custom_call" | custom-call | tf_op jit(solution)/shard_map/pallas_call | solution.py:433
  34.8 0.6 %copy.10 = bf16[64,512]{1,0:T(8,128)(2,1)} copy(bf16[64,512]{1,0:T(8,128)(2,1)S(1)} %shard_map.82) | data formatting | bytes 131072
